TPU v7x, 128 devices: a whole 4x4x4 slice. The times are simulated.
128 devices in a mesh: row: 16 (over y, x), col: 8 (over z, core).
Axes of the slice: x: 4, y: 4, z: 4, core: 2. Of those that a mesh axis runs over, the one named last changes fastest.
Arguments:
- inputs: bfloat16 [1024, 8192], P('col', 'row'), may hold values from -6 to 6
- out_grad: bfloat16 [1024, 8192], P('col', 'row'), may hold values from -1.5 to 1.5
- gate_pre: bfloat16 [1024, 14336], P('row', 'col'), may hold values from -9 to 9
- up_pre: bfloat16 [1024, 14336], P('row', 'col'), may hold values from -6 to 6
- gate_weight: bfloat16 [8192, 14336], P('row', 'col'), may hold values from -0.0625 to 0.0625
- up_weight: bfloat16 [8192, 14336], P('row', 'col'), may hold values from -0.0625 to 0.0625
- down_weight: bfloat16 [14336, 8192], P('col', 'row'), may hold values from -0.046875 to 0.046875
Outputs:
- input_grad: float32 [1024, 8192], P('col', 'row')
- gate_grad: float32 [8192, 14336], P('row', 'col')
- up_grad: float32 [8192, 14336], P('row', 'col')
- down_grad: float32 [14336, 8192], P('col', 'row')
All inputs are finite; a program needn't handle non-finite values.
Results may differ from a plain program's by a relative error of at most 0.0029.
Values may be sent and summed in bfloat16 or wider, within the bound.
A program may use at most 128 MiB of HBM per device.

v0:
```python
import jax
import jax.numpy as jnp
from jax import lax
from jax.sharding import PartitionSpec as P

LEAD_DIMS = (((0,), (0,)), ((), ()))
LAST_DIMS = (((1,), (1,)), ((), ()))


def swiglu_grads(grad_hidden, gate_pre, up_pre):
    gate_val = gate_pre.astype(jnp.float32)
    up_val = up_pre.astype(jnp.float32)
    gate_sig = jax.nn.sigmoid(gate_val)
    hidden = (gate_val * gate_sig * up_val).astype(jnp.bfloat16)
    grad_gate = (grad_hidden * up_val * gate_sig * (1.0 + gate_val * (1.0 - gate_sig))).astype(
        jnp.bfloat16
    )
    grad_up = (grad_hidden * gate_val * gate_sig).astype(jnp.bfloat16)
    return (hidden, grad_gate, grad_up)


def body(inputs, out_grad, gate_pre, up_pre, gate_weight, up_weight, down_weight):
    input_full, grad_full = (
        lax.all_gather(inputs, "col", axis=0, tiled=True),
        lax.all_gather(out_grad, "col", axis=0, tiled=True),
    )
    partial_sum = lax.dot_general(
        grad_full, down_weight, LAST_DIMS, preferred_element_type=jnp.float32
    )
    grad_hidden = lax.psum(partial_sum, "row")
    gate_all, up_all = (
        lax.all_gather(gate_pre, "row", axis=0, tiled=True),
        lax.all_gather(up_pre, "row", axis=0, tiled=True),
    )
    hidden, grad_gate, grad_up = swiglu_grads(grad_hidden, gate_all, up_all)
    total = lax.dot_general(grad_gate, gate_weight, LAST_DIMS, preferred_element_type=jnp.float32)
    input_grad = lax.psum_scatter(
        total + lax.dot_general(grad_up, up_weight, LAST_DIMS, preferred_element_type=jnp.float32),
        "col",
        scatter_dimension=0,
        tiled=True,
    )
    gate_grad = lax.dot_general(
        input_full, grad_gate, LEAD_DIMS, preferred_element_type=jnp.float32
    )
    up_grad = lax.dot_general(input_full, grad_up, LEAD_DIMS, preferred_element_type=jnp.float32)
    down_grad = lax.dot_general(hidden, grad_full, LEAD_DIMS, preferred_element_type=jnp.float32)
    return (input_grad, gate_grad, up_grad, down_grad)


def solution(mesh):
    in_specs = (
        P("col", "row"),
        P("col", "row"),
        P("row", "col"),
        P("row", "col"),
        P("row", "col"),
        P("row", "col"),
        P("col", "row"),
    )
    out_specs = (P("col", "row"), P("row", "col"), P("row", "col"), P("col", "row"))
    return jax.shard_map(body, mesh=mesh, in_specs=in_specs, out_specs=out_specs, check_vma=False)
```

profile of v0, /device:TPU:0, one launch (start us, length us, event | category | flops | bytes accessed | tf_op | source)
XLA Modules:
  0.0 340.9 jit_solution(9743817639233089111)
XLA Ops:
  7.2 0.0 copy-start
  7.2 0.0 all-gather.5.cloned.1.call-start
  7.2 0.7 all-gather.5.cloned.1.call-update
  7.9 0.0 all-gather.7.cloned.1.call-start
  8.0 0.7 all-gather.7.cloned.1.call-update
  8.7 0.0 all-gather.9.cloned.1.call-start
  8.7 0.7 all-gather.9.cloned.1.call-update
  9.4 0.0 all-reduce.2.cloned.1.call-start
  9.4 26.4 %all-gather.5.cloned.1.call-done = bf16[1024,512]{1,0:T(8,128)(2,1)} async-done(((bf16[128,512]{1,0:T(8,128)(2,1)}), bf16[1024,512]{1,0:T(8,128)(2,1)}) %all-gather.5.cloned.1.call-update) | async-done | bytes 1048592 | tf_op jit(solution)/shard_map/all_gather | solution.py:25
  35.8 0.0 copy-done
  35.8 6.4 %fusion.13 = f32[1024,1792]{1,0:T(8,128)} fusion(bf16[1024,512]{1,0:T(8,128)(2,1)} %all-gather.5.cloned.1.call-done, bf16[1792,512]{1,0:T(8,128)(2,1)S(1)} %copy-done), kind=kOutput, calls=%fused_computation.21 | convolution fusion | flops 1879048192 | bytes 10223616 | tf_op jit(solution)/shard_map/dot_general | solution.py:27
  42.2 0.0 all-reduce.2.cloned.1.call-update
  42.2 0.0 all-gather.11.cloned.1.call-start
  42.2 0.5 all-gather.11.cloned.1.call-update
  42.8 0.0 reduce-scatter.2.cloned.1.call-start
  42.8 44.6 %all-gather.7.cloned.1.call-done = bf16[1024,1792]{1,0:T(8,128)(2,1)} async-done(((bf16[64,1792]{1,0:T(8,128)(2,1)}), bf16[1024,1792]{1,0:T(8,128)(2,1)}) %all-gather.7.cloned.1.call-update) | async-done | bytes 3670032 | tf_op jit(solution)/shard_map/all_gather | solution.py:33
  87.4 50.9 %all-gather.9.cloned.1.call-done = bf16[1024,1792]{1,0:T(8,128)(2,1)} async-done(((bf16[64,1792]{1,0:T(8,128)(2,1)}), bf16[1024,1792]{1,0:T(8,128)(2,1)}) %all-gather.9.cloned.1.call-update) | async-done | bytes 3670032 | tf_op jit(solution)/shard_map/all_gather | solution.py:32
  138.3 133.8 %all-reduce.2.cloned.1.call-done = f32[1024,1792]{1,0:T(8,128)} async-done(((f32[1024,1792]{1,0:T(8,128)}), f32[1024,1792]{1,0:T(8,128)}) %all-reduce.2.cloned.1.call-update) | async-done | bytes 7340048 | tf_op jit(solution)/shard_map/psum | solution.py:30
  272.2 7.1 %fusion.9 = (bf16[1024,1792]{1,0:T(8,128)(2,1)S(1)}, bf16[1024,1792]{1,0:T(8,128)(2,1)S(1)}) fusion(f32[1024,1792]{1,0:T(8,128)} %all-reduce.2.cloned.1.call-done, bf16[1024,1792]{1,0:T(8,128)(2,1)} %all-gather.9.cloned.1.call-done, bf16[1024,1792]{1,0:T(8,128)(2,1)} %all-gather.7.cloned.1.call-done), kind=kLoop, calls=%fused_computation.15 | loop fusion | flops 27525120 | bytes 22020096 | tf_op jit(solution)/shard_map/convert_element_type | solution.py:18
  279.3 0.0 copy-start.2
  279.3 0.0 copy-start.4
  279.4 2.1 fusion.14
  281.5 1.1 copy-done.1
  282.5 3.5 %convolution_add_fusion = f32[1024,512]{1,0:T(8,128)} fusion(f32[1024,512]{1,0:T(8,128)S(1)} %fusion.14, bf16[1024,1792]{1,0:T(8,128)(2,1)S(1)} %get-tuple-element.8, bf16[512,1792]{1,0:T(8,128)(2,1)S(1)} %copy-done.4), kind=kOutput, calls=%fused_computation.19 | convolution fusion | flops 1879572480 | bytes 9699328 | tf_op jit(solution)/shard_map/dot_general | solution.py:38
  286.0 0.0 reduce-scatter.2.cloned.1.call-update
  286.0 7.8 %fusion.10 = f32[1792,512]{1,0:T(8,128)} fusion(bf16[1024,512]{1,0:T(8,128)(2,1)S(1)} %copy-done.5, bf16[1024,1792]{1,0:T(8,128)(2,1)} %all-gather.7.cloned.1.call-done, bf16[1024,1792]{1,0:T(8,128)(2,1)} %all-gather.9.cloned.1.call-done), kind=kOutput, calls=%fused_computation.16 | convolution fusion | flops 1893728256 | bytes 12058624 | tf_op jit(solution)/shard_map/dot_general | solution.py:47
  293.9 3.4 all-gather.11.cloned.1.call-done
  297.3 6.3 %convolution_bitcast_fusion.1 = f32[512,1792]{0,1:T(8,128)} fusion(bf16[1024,1792]{1,0:T(8,128)(2,1)} %copy-done.2, bf16[1024,512]{1,0:T(8,128)(2,1)} %all-gather.11.cloned.1.call-done), kind=kOutput, calls=%fused_computation.18 | convolution fusion | flops 1879048192 | bytes 8388608 | tf_op jit(solution)/shard_map/dot_general | solution.py:43
  303.5 5.2 %copy.11 = f32[512,1792]{1,0:T(8,128)} copy(f32[512,1792]{0,1:T(8,128)} %convolution_bitcast_fusion.1) | data formatting | bytes 7340032
  308.7 6.0 %convolution_bitcast_fusion = f32[512,1792]{0,1:T(8,128)} fusion(bf16[1024,1792]{1,0:T(8,128)(2,1)} %copy-done.1, bf16[1024,512]{1,0:T(8,128)(2,1)S(1)} %copy-done.6), kind=kOutput, calls=%fused_computation.17 | convolution fusion | flops 1879048192 | bytes 8388608 | tf_op jit(solution)/shard_map/dot_general | solution.py:46
  314.7 5.2 %copy.12 = f32[512,1792]{1,0:T(8,128)} copy(f32[512,1792]{0,1:T(8,128)} %convolution_bitcast_fusion) | data formatting | bytes 7340032
  319.9 14.1 %reduce-scatter.2.cloned.1.call-done = f32[128,512]{1,0:T(8,128)} async-done(((f32[1024,512]{1,0:T(8,128)}), f32[128,512]{1,0:T(8,128)}) %reduce-scatter.2.cloned.1.call-update) | async-done | bytes 262160 | tf_op jit(solution)/shard_map/reduce_scatter | solution.py:37
  (9 shorter events, 0.0 us)
Async XLA Ops:
  7.2 28.6 %copy-start = (bf16[1792,512]{1,0:T(8,128)(2,1)S(1)}, bf16[1792,512]{1,0:T(8,128)(2,1)}, u32[]{:S(2)}) copy-start(bf16[1792,512]{1,0:T(8,128)(2,1)} %param.13) | copy-start | bytes 5505028
  7.2 28.6 %all-gather.5.cloned.1.call-start = ((), (), s32[]{:S(2)}) async-start(), calls=%async_computation.1 | async-start | bytes 1179648 | tf_op jit(solution)/shard_map/all_gather | solution.py:25
  7.9 79.5 %all-gather.7.cloned.1.call-start = ((), (), s32[]{:S(2)}) async-start(), calls=%async_computation.3 | async-start | bytes 3899392 | tf_op jit(solution)/shard_map/all_gather | solution.py:33
  8.7 129.7 %all-gather.9.cloned.1.call-start = ((), (), s32[]{:S(2)}) async-start(), calls=%async_computation.4 | async-start | bytes 3899392 | tf_op jit(solution)/shard_map/all_gather | solution.py:32
  9.4 262.8 %all-reduce.2.cloned.1.call-start = ((), (), s32[]{:S(2)}) async-start(), calls=%async_computation.2 | async-start | bytes 14680064 | tf_op jit(solution)/shard_map/psum | solution.py:30
  42.2 255.1 %all-gather.11.cloned.1.call-start = ((), (), s32[]{:S(2)}) async-start(), calls=%async_computation.6 | async-start | bytes 1179648 | tf_op jit(solution)/shard_map/all_gather | solution.py:24
  42.8 291.3 %reduce-scatter.2.cloned.1.call-start = ((), (), s32[]{:S(2)}) async-start(), calls=%async_computation.5 | async-start | bytes 2359296 | tf_op jit(solution)/shard_map/reduce_scatter | solution.py:37
  272.2 7.2 %copy-start.3 = (bf16[512,1792]{1,0:T(8,128)(2,1)S(1)}, bf16[512,1792]{1,0:T(8,128)(2,1)}, u32[]{:S(2)}) copy-start(bf16[512,1792]{1,0:T(8,128)(2,1)} %param.11) | copy-start | bytes 5505028
  279.3 2.1 copy-start.2
  279.3 3.2 copy-start.1
  279.3 3.2 copy-start.4
  282.5 3.5 %copy-start.5 = (bf16[1024,512]{1,0:T(8,128)(2,1)S(1)}, bf16[1024,512]{1,0:T(8,128)(2,1)}, u32[]{:S(2)}) copy-start(bf16[1024,512]{1,0:T(8,128)(2,1)} %all-gather.5.cloned.1.call-done) | copy-start | bytes 3145732
  303.5 5.2 %copy-start.6 = (bf16[1024,512]{1,0:T(8,128)(2,1)S(1)}, bf16[1024,512]{1,0:T(8,128)(2,1)}, u32[]{:S(2)}) copy-start(bf16[1024,512]{1,0:T(8,128)(2,1)} %all-gather.11.cloned.1.call-done) | copy-start | bytes 3145732
Sparse Core Ops, SparseCore 0:
  9.7 26.0 all-gather.4
  37.9 49.4 all-gather.6
  89.5 48.7 all-gather.8
  141.6 130.4 all-reduce.1
  273.8 23.3 all-gather.10
  300.2 33.7 reduce-scatter.1
where the time goes:
time: 341 us
  waiting for transfers between devices  276 us (81%)
  matrix products  32 us (9%)
  between operations  14.2 us (4%)
  local copies, waits for them, and re-layouts  11.4 us (3%)
  other arithmetic  7.15 us (2%)
    psum x1, waiting for transfers between devices, body(): grad_hidden = lax.psum(partial_sum, 'row')  134 us
    all_gather x1, waiting for transfers between devices, body(): lax.all_gather(gate_pre, 'row', axis=0, tiled=True)  50.9 us
    all_gather x1, waiting for transfers between devices, body(): lax.all_gather(up_pre, 'row', axis=0, tiled=True)  44.6 us
    all_gather x1, waiting for transfers between devices, body(): lax.all_gather(out_grad, 'col', axis=0, tiled=True)  26.4 us
    reduce_scatter x1, waiting for transfers between devices, body(): lax.psum_scatter(total + lax.dot_general(grad_up, up_weight, LAST_DIMS, p...  14.1 us
    unnamed x16, local copies, waits for them, and re-layouts  11.4 us
    dot_general x1, matrix products, body(): lax.dot_general(hidden, grad_full, LEAD_DIMS, preferred_element_type=jnp....  7.83 us
    convert_element_type x1, other arithmetic, swiglu_grads(): grad_up = (grad_hidden * gate_val * gate_sig).astype(jnp.bfloat16)  7.15 us
  transfers between devices with their start and end apart: 6, of which 6 were waited for; matrix products, arithmetic and copies ran while one was open for 15% of the time, Pallas kernels for 0%

commit v1 on v0

--- a/solution.py
+++ b/solution.py
@@ -5,6 +5,27 @@
 
 LEAD_DIMS = (((0,), (0,)), ((), ()))
 LAST_DIMS = (((1,), (1,)), ((), ()))
+
+
+def gather_around(x, axis, dim):
+    size, index, rows = (lax.axis_size(axis), lax.axis_index(axis), x.shape[dim])
+    forward = [(i, (i + 1) % size) for i in range(size)]
+    behind = [(i, (i - 1) % size) for i in range(size)]
+    whole = jnp.zeros((*x.shape[:dim], size * rows, *x.shape[dim + 1 :]), x.dtype)
+    whole = lax.dynamic_update_slice_in_dim(whole, x, index * rows, axis=dim)
+    from_left = from_right = x
+    half = size // 2
+    for step in range(1, half + 1):
+        from_left = lax.ppermute(from_left, axis, forward)
+        whole = lax.dynamic_update_slice_in_dim(
+            whole, from_left, (index - step) % size * rows, axis=dim
+        )
+        if step < size - half:
+            from_right = lax.ppermute(from_right, axis, behind)
+            whole = lax.dynamic_update_slice_in_dim(
+                whole, from_right, (index + step) % size * rows, axis=dim
+            )
+    return whole
 
 
 def swiglu_grads(grad_hidden, gate_pre, up_pre):
@@ -22,7 +43,7 @@
 def body(inputs, out_grad, gate_pre, up_pre, gate_weight, up_weight, down_weight):
     input_full, grad_full = (
         lax.all_gather(inputs, "col", axis=0, tiled=True),
-        lax.all_gather(out_grad, "col", axis=0, tiled=True),
+        gather_around(out_grad, "col", 0),
     )
     partial_sum = lax.dot_general(
         grad_full, down_weight, LAST_DIMS, preferred_element_type=jnp.float32

time: 341 us -> 316 us (0.927)
  waiting for transfers between devices: 276 us -> 241 us
  starting transfers between devices: 0.23 us -> 9.92 us
    all_gather x1, waiting for transfers between devices: 50.9 us -> 24.2 us  [body(): lax.all_gather(gate_pre, 'row', axis=0, tiled=True)]
    all_gather x1 -> x0, waiting for transfers between devices: 26.4 us -> none  [body(): lax.all_gather(out_grad, 'col', axis=0, tiled=True)]
    ppermute x0 -> x7, waiting for transfers between devices: none -> 12.6 us  [the longest x4 12.6 us: gather_around(): from_left = lax.ppermute(from_left, axis, forward)]
    ppermute x0 -> x7, starting transfers between devices: none -> 9.54 us  [the longest x3 9.51 us: gather_around(): from_right = lax.ppermute(from_right, axis, behind)]
    all_gather x1, waiting for transfers between devices: 44.6 us -> 50.9 us  [body(): lax.all_gather(up_pre, 'row', axis=0, tiled=True)]
    unnamed x16 -> x14, local copies, waits for them, and re-layouts: 11.4 us -> 11.4 us
  transfers between devices with their start and end apart: 6 -> 12, of which waited for: 6 -> 9; matrix products, arithmetic and copies ran while one was open for 15% -> 16% of each run, Pallas kernels for 0% -> 0%
where the time goes in v1:
time: 316 us; the launch traced here: 315 us
  waiting for transfers between devices  241 us (76%)
  matrix products  30.8 us (10%)
  between operations  13.9 us (4%)
  local copies, waits for them, and re-layouts  12.5 us (4%)
  starting transfers between devices  9.92 us (3%)
  other arithmetic  7.15 us (2%)
    psum x1, waiting for transfers between devices, body(): grad_hidden = lax.psum(partial_sum, 'row')  134 us
    all_gather x1, waiting for transfers between devices, body(): lax.all_gather(up_pre, 'row', axis=0, tiled=True)  50.9 us
    all_gather x1, waiting for transfers between devices, body(): lax.all_gather(gate_pre, 'row', axis=0, tiled=True)  24.2 us
    reduce_scatter x1, waiting for transfers between devices, body(): lax.psum_scatter(total + lax.dot_general(grad_up, up_weight, LAST_DIMS, p...  14.1 us
    ppermute x4, waiting for transfers between devices, gather_around(): from_left = lax.ppermute(from_left, axis, forward)  12.6 us
    unnamed x14, local copies, waits for them, and re-layouts  11.4 us
    ppermute x3, starting transfers between devices, gather_around(): from_right = lax.ppermute(from_right, axis, behind)  9.51 us
    dot_general x1, matrix products, body(): lax.dot_general(hidden, grad_full, LEAD_DIMS, preferred_element_type=jnp....  7.82 us
  transfers between devices with their start and end apart: 12, of which 9 were waited for; matrix products, arithmetic and copies ran while one was open for 16% of the time, Pallas kernels for 0%

profile of v1, /device:TPU:0, one launch (start us, length us, event | category | flops | bytes accessed | tf_op | source)
XLA Modules:
  0.0 315.5 jit_solution(10186230406202325329)
XLA Ops:
  7.2 0.0 all-gather.6.cloned.1.call-start
  7.2 0.7 all-gather.6.cloned.1.call-update
  7.9 0.0 all-gather.4.cloned.1.call-start
  8.0 0.7 all-gather.4.cloned.1.call-update
  8.7 0.0 all-reduce.2.cloned.1.call-start
  8.7 3.6 %collective-permute-start.1 = (bf16[128,512]{1,0:T(8,128)(2,1)}, bf16[128,512]{1,0:T(8,128)(2,1)S(1)}, u32[]{:S(2)}, u32[]{:S(2)}) collective-permute-start(bf16[128,512]{1,0:T(8,128)(2,1)} %param.8), channel_id=1, source_target_pairs={{0,7},{1,0},{2,1},{3,2},{4,3},{5,4},{6,5},{7,6},{8,15},{9,8},{10,9... | collective-permute-start | bytes 393224 | tf_op jit(solution)/shard_map/ppermute | solution.py:24
  12.3 0.1 broadcast_in_dim.3
  12.4 0.9 constant_dynamic-update-slice_fusion.7
  13.3 1.8 collective-permute-done
  15.2 3.0 collective-permute-start.3
  18.2 2.6 collective-permute-done.2
  20.8 3.0 collective-permute-start.5
  23.8 2.6 collective-permute-done.4
  26.4 5.5 %collective-permute-done.6 = bf16[128,512]{1,0:T(8,128)(2,1)S(1)} collective-permute-done((bf16[128,512]{1,0:T(8,128)(2,1)S(1)}, bf16[128,512]{1,0:T(8,128)(2,1)S(1)}, u32[]{:S(2)}, u32[]{:S(2)}) %collective-permute-start.6) | collective-permute-done | bytes 131104 | tf_op jit(solution)/shard_map/ppermute | solution.py:19
  32.0 5.1 %fusion.13 = f32[1024,1792]{1,0:T(8,128)} fusion(bf16[1024,512]{1,0:T(8,128)(2,1)S(1)} %constant_dynamic-update-slice_fusion, bf16[1792,512]{1,0:T(8,128)(2,1)S(1)} %copy-done), kind=kOutput, calls=%fused_computation.29 | convolution fusion | flops 1879048192 | bytes 10223616 | tf_op jit(solution)/shard_map/dot_general | solution.py:48
  37.1 0.0 all-gather.8.cloned.1.call-start
  37.2 0.5 all-gather.8.cloned.1.call-update
  37.7 0.2 reduce-scatter.2.cloned.1.call-start
  38.0 24.2 %all-gather.6.cloned.1.call-done = bf16[1024,1792]{1,0:T(8,128)(2,1)} async-done(((bf16[64,1792]{1,0:T(8,128)(2,1)}), bf16[1024,1792]{1,0:T(8,128)(2,1)}) %all-gather.6.cloned.1.call-update) | async-done | bytes 3670032 | tf_op jit(solution)/shard_map/all_gather | solution.py:53
  62.2 50.9 %all-gather.4.cloned.1.call-done = bf16[1024,1792]{1,0:T(8,128)(2,1)} async-done(((bf16[64,1792]{1,0:T(8,128)(2,1)}), bf16[1024,1792]{1,0:T(8,128)(2,1)}) %all-gather.4.cloned.1.call-update) | async-done | bytes 3670032 | tf_op jit(solution)/shard_map/all_gather | solution.py:54
  113.1 134.0 %all-reduce.2.cloned.1.call-done = f32[1024,1792]{1,0:T(8,128)} async-done(((f32[1024,1792]{1,0:T(8,128)}), f32[1024,1792]{1,0:T(8,128)}) %all-reduce.2.cloned.1.call-update) | async-done | bytes 7340048 | tf_op jit(solution)/shard_map/psum | solution.py:51
  247.1 7.1 %fusion.9 = (bf16[1024,1792]{1,0:T(8,128)(2,1)S(1)}, bf16[1024,1792]{1,0:T(8,128)(2,1)S(1)}) fusion(f32[1024,1792]{1,0:T(8,128)} %all-reduce.2.cloned.1.call-done, bf16[1024,1792]{1,0:T(8,128)(2,1)} %all-gather.6.cloned.1.call-done, bf16[1024,1792]{1,0:T(8,128)(2,1)} %all-gather.4.cloned.1.call-done), kind=kLoop, calls=%fused_computation.15 | loop fusion | flops 27525120 | bytes 22020096 | tf_op jit(solution)/shard_map/convert_element_type | solution.py:39
  254.3 2.1 fusion.14
  256.4 1.1 copy-done.1
  257.5 3.5 %convolution_add_fusion = f32[1024,512]{1,0:T(8,128)} fusion(f32[1024,512]{1,0:T(8,128)S(1)} %fusion.14, bf16[1024,1792]{1,0:T(8,128)(2,1)S(1)} %get-tuple-element.8, bf16[512,1792]{1,0:T(8,128)(2,1)S(1)} %copy-done.4), kind=kOutput, calls=%fused_computation.19 | convolution fusion | flops 1879572480 | bytes 9699328 | tf_op jit(solution)/shard_map/dot_general | solution.py:59
  261.0 7.8 %fusion.10 = f32[1792,512]{1,0:T(8,128)} fusion(bf16[1024,512]{1,0:T(8,128)(2,1)S(1)} %constant_dynamic-update-slice_fusion, bf16[1024,1792]{1,0:T(8,128)(2,1)} %all-gather.4.cloned.1.call-done, bf16[1024,1792]{1,0:T(8,128)(2,1)} %all-gather.6.cloned.1.call-done), kind=kOutput, calls=%fused_computation.16 | convolution fusion | flops 1893728256 | bytes 12058624 | tf_op jit(solution)/shard_map/dot_general | solution.py:68
  268.8 3.4 %all-gather.8.cloned.1.call-done = bf16[1024,512]{1,0:T(8,128)(2,1)} async-done(((bf16[128,512]{1,0:T(8,128)(2,1)}), bf16[1024,512]{1,0:T(8,128)(2,1)}) %all-gather.8.cloned.1.call-update) | async-done | bytes 1048592 | tf_op jit(solution)/shard_map/all_gather | solution.py:45
  272.2 6.3 %convolution_bitcast_fusion.1 = f32[512,1792]{0,1:T(8,128)} fusion(bf16[1024,1792]{1,0:T(8,128)(2,1)} %copy-done.2, bf16[1024,512]{1,0:T(8,128)(2,1)} %all-gather.8.cloned.1.call-done), kind=kOutput, calls=%fused_computation.18 | convolution fusion | flops 1879048192 | bytes 8388608 | tf_op jit(solution)/shard_map/dot_general | solution.py:64
  278.5 5.2 %copy.11 = f32[512,1792]{1,0:T(8,128)} copy(f32[512,1792]{0,1:T(8,128)} %convolution_bitcast_fusion.1) | data formatting | bytes 7340032
  283.7 6.0 %convolution_bitcast_fusion = f32[512,1792]{0,1:T(8,128)} fusion(bf16[1024,1792]{1,0:T(8,128)(2,1)} %copy-done.1, bf16[1024,512]{1,0:T(8,128)(2,1)S(1)} %copy-done.5), kind=kOutput, calls=%fused_computation.17 | convolution fusion | flops 1879048192 | bytes 8388608 | tf_op jit(solution)/shard_map/dot_general | solution.py:67
  289.7 5.1 %copy.12 = f32[512,1792]{1,0:T(8,128)} copy(f32[512,1792]{0,1:T(8,128)} %convolution_bitcast_fusion) | data formatting | bytes 7340032
  294.9 14.1 %reduce-scatter.2.cloned.1.call-done = f32[128,512]{1,0:T(8,128)} async-done(((f32[1024,512]{1,0:T(8,128)}), f32[128,512]{1,0:T(8,128)}) %reduce-scatter.2.cloned.1.call-update) | async-done | bytes 262160 | tf_op jit(solution)/shard_map/reduce_scatter | solution.py:58
  (27 shorter events, 0.2 us)
Async XLA Ops:
  7.2 24.8 %copy-start = (bf16[1792,512]{1,0:T(8,128)(2,1)S(1)}, bf16[1792,512]{1,0:T(8,128)(2,1)}, u32[]{:S(2)}) copy-start(bf16[1792,512]{1,0:T(8,128)(2,1)} %param.13) | copy-start | bytes 5505028
  7.2 55.0 %all-gather.6.cloned.1.call-start = ((), (), s32[]{:S(2)}) async-start(), calls=%async_computation.3 | async-start | bytes 3899392 | tf_op jit(solution)/shard_map/all_gather | solution.py:53
  7.9 105.2 %all-gather.4.cloned.1.call-start = ((), (), s32[]{:S(2)}) async-start(), calls=%async_computation.2 | async-start | bytes 3899392 | tf_op jit(solution)/shard_map/all_gather | solution.py:54
  8.7 238.5 %all-reduce.2.cloned.1.call-start = ((), (), s32[]{:S(2)}) async-start(), calls=%async_computation.1 | async-start | bytes 14680064 | tf_op jit(solution)/shard_map/psum | solution.py:51
  8.7 6.4 %collective-permute-start = (bf16[128,512]{1,0:T(8,128)(2,1)}, bf16[128,512]{1,0:T(8,128)(2,1)S(1)}, u32[]{:S(2)}, u32[]{:S(2)}) collective-permute-start(bf16[128,512]{1,0:T(8,128)(2,1)} %param.8), channel_id=1, source_target_pairs={{0,1},{1,2},{2,3},{3,4},{4,5},{5,6},{6,7},{7,0},{8,9},{9,10},{10,1... | collective-permute-start | bytes 393224 | tf_op jit(solution)/shard_map/ppermute | solution.py:19
  8.7 6.4 %collective-permute-start.1 = (bf16[128,512]{1,0:T(8,128)(2,1)}, bf16[128,512]{1,0:T(8,128)(2,1)S(1)}, u32[]{:S(2)}, u32[]{:S(2)}) collective-permute-start(bf16[128,512]{1,0:T(8,128)(2,1)} %param.8), channel_id=1, source_target_pairs={{0,7},{1,0},{2,1},{3,2},{4,3},{5,4},{6,5},{7,6},{8,15},{9,8},{10,9... | collective-permute-start | bytes 393224 | tf_op jit(solution)/shard_map/ppermute | solution.py:24
  15.1 5.6 %collective-permute-start.2 = (bf16[128,512]{1,0:T(8,128)(2,1)S(1)}, bf16[128,512]{1,0:T(8,128)(2,1)S(1)}, u32[]{:S(2)}, u32[]{:S(2)}) collective-permute-start(bf16[128,512]{1,0:T(8,128)(2,1)S(1)} %collective-permute-done), channel_id=1, source_target_pairs={{0,1},{1,2},{2,3},{3,4},{4,5},{5,6},{6,7},{7,0},{8,9},{9,10},{10,1... | collective-permute-start | bytes 393224 | tf_op jit(solution)/shard_map/ppermute | solution.py:19
  15.2 5.6 %collective-permute-start.3 = (bf16[128,512]{1,0:T(8,128)(2,1)S(1)}, bf16[128,512]{1,0:T(8,128)(2,1)S(1)}, u32[]{:S(2)}, u32[]{:S(2)}) collective-permute-start(bf16[128,512]{1,0:T(8,128)(2,1)S(1)} %collective-permute-done.1), channel_id=1, source_target_pairs={{0,7},{1,0},{2,1},{3,2},{4,3},{5,4},{6,5},{7,6},{8,15},{9,8},{10,9... | collective-permute-start | bytes 393224 | tf_op jit(solution)/shard_map/ppermute | solution.py:24
  20.8 5.6 %collective-permute-start.4 = (bf16[128,512]{1,0:T(8,128)(2,1)S(1)}, bf16[128,512]{1,0:T(8,128)(2,1)S(1)}, u32[]{:S(2)}, u32[]{:S(2)}) collective-permute-start(bf16[128,512]{1,0:T(8,128)(2,1)S(1)} %collective-permute-done.2), channel_id=1, source_target_pairs={{0,1},{1,2},{2,3},{3,4},{4,5},{5,6},{6,7},{7,0},{8,9},{9,10},{10,1... | collective-permute-start | bytes 393224 | tf_op jit(solution)/shard_map/ppermute | solution.py:19
  20.8 5.6 %collective-permute-start.5 = (bf16[128,512]{1,0:T(8,128)(2,1)S(1)}, bf16[128,512]{1,0:T(8,128)(2,1)S(1)}, u32[]{:S(2)}, u32[]{:S(2)}) collective-permute-start(bf16[128,512]{1,0:T(8,128)(2,1)S(1)} %collective-permute-done.3), channel_id=1, source_target_pairs={{0,7},{1,0},{2,1},{3,2},{4,3},{5,4},{6,5},{7,6},{8,15},{9,8},{10,9... | collective-permute-start | bytes 393224 | tf_op jit(solution)/shard_map/ppermute | solution.py:24
  26.4 5.6 %collective-permute-start.6 = (bf16[128,512]{1,0:T(8,128)(2,1)S(1)}, bf16[128,512]{1,0:T(8,128)(2,1)S(1)}, u32[]{:S(2)}, u32[]{:S(2)}) collective-permute-start(bf16[128,512]{1,0:T(8,128)(2,1)S(1)} %collective-permute-done.4), channel_id=1, source_target_pairs={{0,1},{1,2},{2,3},{3,4},{4,5},{5,6},{6,7},{7,0},{8,9},{9,10},{10,1... | collective-permute-start | bytes 393224 | tf_op jit(solution)/shard_map/ppermute | solution.py:19
  37.1 235.1 %all-gather.8.cloned.1.call-start = ((), (), s32[]{:S(2)}) async-start(), calls=%async_computation.5 | async-start | bytes 1179648 | tf_op jit(solution)/shard_map/all_gather | solution.py:45
  37.7 271.2 %reduce-scatter.2.cloned.1.call-start = ((), (), s32[]{:S(2)}) async-start(), calls=%async_computation.4 | async-start | bytes 2359296 | tf_op jit(solution)/shard_map/reduce_scatter | solution.py:58
  247.1 7.2 %copy-start.3 = (bf16[512,1792]{1,0:T(8,128)(2,1)S(1)}, bf16[512,1792]{1,0:T(8,128)(2,1)}, u32[]{:S(2)}) copy-start(bf16[512,1792]{1,0:T(8,128)(2,1)} %param.11) | copy-start | bytes 5505028
  254.3 2.1 copy-start.2
  254.3 3.2 %copy-start.1 = (bf16[1024,1792]{1,0:T(8,128)(2,1)}, bf16[1024,1792]{1,0:T(8,128)(2,1)S(1)}, u32[]{:S(2)}) copy-start(bf16[1024,1792]{1,0:T(8,128)(2,1)S(1)} %get-tuple-element.8) | copy-start | bytes 11010052
  254.3 3.2 %copy-start.4 = (bf16[512,1792]{1,0:T(8,128)(2,1)S(1)}, bf16[512,1792]{1,0:T(8,128)(2,1)}, u32[]{:S(2)}) copy-start(bf16[512,1792]{1,0:T(8,128)(2,1)} %param.12) | copy-start | bytes 5505028
  278.5 5.2 %copy-start.5 = (bf16[1024,512]{1,0:T(8,128)(2,1)S(1)}, bf16[1024,512]{1,0:T(8,128)(2,1)}, u32[]{:S(2)}) copy-start(bf16[1024,512]{1,0:T(8,128)(2,1)} %all-gather.8.cloned.1.call-done) | copy-start | bytes 3145732
Sparse Core Ops, SparseCore 0:
  10.1 51.9 all-gather.5
  64.3 48.7 all-gather.3
  116.6 130.5 all-reduce.1
  248.8 23.3 all-gather.7
  275.2 33.7 reduce-scatter.1
